TPU v7x, 256 devices: a whole 4x4x8 slice. The times are simulated.
256 devices in a mesh: ctx: 16 (over z, y_hi), head: 16 (over y_lo, x, core).
Axes of the slice: x: 4, y: 4 (y_hi: 2, y_lo: 2; y = y_hi * 2 + y_lo), z: 8, core: 2. Of those that a mesh axis runs over, the one named last changes fastest.
Arguments:
- main_query: bfloat16 [4096, 128, 576], P('ctx', 'head'), may hold values from -12 to 12
- key_latent: bfloat16 [12288, 576], P('ctx'), may hold values from -6 to 6
- index_query: bfloat16 [4096, 64, 128], P('ctx', 'head'), may hold values from -0.53033009 to 0.53033009
- index_key: bfloat16 [12288, 128], P('ctx'), may hold values from -6 to 6
- index_weight: float32 [4096, 64], P('ctx', 'head'), may hold values from -1.6 to 1.6
- selection: int32 [16, 16], replicated, may hold values from 0 to 95, as said below
- loss_grad: float32 [4096], P('ctx'), may hold values from 8 to 64
Outputs:
- query_grad: float32 [4096, 64, 128], P('ctx', 'head')
- weight_grad: float32 [4096, 64], P('ctx', 'head')
- key_grad: float32 [12288, 128], P(('ctx', 'head'))
- query_loss: float32 [4096], P('ctx')
Inputs may be any that keep to these rules, and one draw needn't show every extreme that they name: `selection`: row b lists 16 different key tiles, all at or below key tile 16 * 4 + 2 * b + 1, and includes the 2 tiles from 16 * 4 + 2 * b upward. Within any aligned group of 6 tiles (the keys of one device) a row names at most 3 tiles; in every draw one group that lies below all queries is named exactly 3 times by every row.
All inputs are finite; a program needn't handle non-finite values.
Results may differ from a plain program's by a relative error of at most 0.012.
Values may be sent and summed in bfloat16 or wider, within the bound.
No kernel may reach another device: no remote copies, remote signals or barrier semaphores. Data moves between devices by JAX's collectives and lax.ppermute only.
A program may use at most 128 MiB of HBM per device.

v0:
```python
import jax
import jax.numpy as jnp
from jax import lax
from jax.sharding import PartitionSpec as P

TILE = 128
MLA_HEADS = 128


score_scale = 192.0 ** (-0.5)
far_below = -1e30


def masked_softmax(raw_scores, allowed):
    masked = jnp.where(allowed, raw_scores, far_below)
    row_max = jnp.max(masked, axis=-1, keepdims=True)
    weights = jnp.where(allowed, jnp.exp(raw_scores - row_max), 0.0)
    return weights / jnp.sum(weights, axis=-1, keepdims=True)


def finish_scores(total_target, total_score, allowed, grad_rows):
    target = total_target / MLA_HEADS
    masked = jnp.where(allowed, total_score, far_below)
    row_max = jnp.max(masked, axis=-1, keepdims=True)
    weights = jnp.where(allowed, jnp.exp(total_score - row_max), 0.0)
    row_sum = jnp.sum(weights, axis=-1, keepdims=True)
    index_prob = weights / row_sum
    log_prob = total_score - row_max - jnp.log(row_sum)
    positive = target > 0
    self_term = jnp.where(positive, target * jnp.log(jnp.where(positive, target, 1.0)), 0.0)
    loss_rows = jnp.sum(jnp.where(allowed, self_term - target * log_prob, 0.0), axis=-1)
    score_grad = grad_rows[:, None] * jnp.where(allowed, index_prob - target, 0.0)
    return (score_grad, loss_rows)


def keep_state(current):
    return current


def body(main_query, key_latent, index_query, index_key, index_weight, selection, loss_grad):
    ctx_index = lax.axis_index("ctx")
    ctx_count = lax.axis_size("ctx")
    query_rows, main_local, lat_width = main_query.shape
    index_local = index_query.shape[1]
    key_tiles = key_latent.shape[0] // TILE
    idx_width = index_key.shape[1]
    picked = lax.dynamic_index_in_dim(selection, ctx_index, 0, keepdims=False)
    sel_count = picked.shape[0]
    key_span = sel_count * TILE
    context = key_tiles * TILE * ctx_count
    query_pos = context - query_rows * ctx_count + ctx_index * query_rows + jnp.arange(query_rows)
    key_pos = (picked[:, None] * TILE + jnp.arange(TILE)[None, :]).reshape(key_span)
    allowed = key_pos[None, :] <= query_pos[:, None]
    latent_tiles = key_latent.reshape(key_tiles, TILE, lat_width)
    index_tiles = index_key.reshape(key_tiles, TILE, idx_width)
    empty_latent = jnp.zeros((sel_count, TILE, lat_width), jnp.bfloat16)
    empty_index = jnp.zeros((sel_count, TILE, idx_width), jnp.bfloat16)
    latent_piece = lax.all_gather(latent_tiles, "ctx", axis=0, tiled=True)
    index_piece = lax.all_gather(index_tiles, "ctx", axis=0, tiled=True)
    piece_tiles = latent_piece.shape[0]

    def place_tile(slot_index, state_pair):
        local_tile = picked[slot_index]
        inside = (local_tile >= 0) & (local_tile < piece_tiles)
        tile_spot = jnp.clip(local_tile, 0, piece_tiles - 1)

        def write_tile(current):
            new_latent = lax.dynamic_update_slice_in_dim(
                current[0], lax.dynamic_slice_in_dim(latent_piece, tile_spot, 1, 0), slot_index, 0
            )
            new_index = lax.dynamic_update_slice_in_dim(
                current[1], lax.dynamic_slice_in_dim(index_piece, tile_spot, 1, 0), slot_index, 0
            )
            return (new_latent, new_index)

        return lax.cond(inside, write_tile, keep_state, state_pair)

    got_latent, got_index = lax.fori_loop(0, sel_count, place_tile, (empty_latent, empty_index))
    keys_latent = got_latent.reshape(key_span, lat_width)
    keys_index = got_index.reshape(key_span, idx_width)
    head_block = 2

    def add_heads(block_step, summed):
        head_rows = lax.dynamic_slice_in_dim(main_query, block_step * head_block, head_block, 1)
        head_rows = head_rows.reshape(query_rows * head_block, lat_width)
        raw_scores = (
            lax.dot_general(
                head_rows, keys_latent, (((1,), (1,)), ((), ())), preferred_element_type=jnp.float32
            )
            * score_scale
        )
        attend = masked_softmax(
            raw_scores.reshape(query_rows, head_block, key_span), allowed[:, None, :]
        )
        return summed + jnp.sum(attend, axis=1)

    target_part = lax.fori_loop(
        0, main_local // head_block, add_heads, jnp.zeros((query_rows, key_span), jnp.float32)
    )
    query_flat = index_query.reshape(query_rows * index_local, idx_width)
    logits = lax.dot_general(
        query_flat, keys_index, (((1,), (1,)), ((), ())), preferred_element_type=jnp.float32
    ).reshape(query_rows, index_local, key_span)
    lifted = jnp.maximum(logits, 0.0)
    score_part = jnp.sum(index_weight[:, :, None] * lifted, axis=1)
    total_target, total_score = lax.psum((target_part, score_part), "head")
    score_grad, query_loss = finish_scores(total_target, total_score, allowed, loss_grad)
    coefficient = (score_grad[:, None, :] * index_weight[:, :, None] * (logits > 0)).astype(
        jnp.bfloat16
    )
    coef_flat = coefficient.reshape(query_rows * index_local, key_span)
    query_grad = jnp.dot(coef_flat, keys_index, preferred_element_type=jnp.float32)
    query_grad = query_grad.reshape(query_rows, index_local, idx_width)
    weight_grad = jnp.sum(score_grad[:, None, :] * lifted, axis=2)
    key_part = lax.dot_general(
        coef_flat, query_flat, (((0,), (0,)), ((), ())), preferred_element_type=jnp.float32
    ).reshape(sel_count, TILE, idx_width)
    dense_term = jnp.zeros((ctx_count * key_tiles, TILE, idx_width), jnp.float32)
    dense_term = dense_term.at[picked].add(key_part).reshape(context, idx_width)
    key_grad = lax.psum_scatter(dense_term, ("ctx", "head"), scatter_dimension=0, tiled=True)
    return (query_grad, weight_grad, key_grad, query_loss)


def solution(mesh):
    return jax.shard_map(
        body,
        mesh=mesh,
        in_specs=(
            P("ctx", "head", None),
            P("ctx", None),
            P("ctx", "head", None),
            P("ctx", None),
            P("ctx", "head"),
            P(),
            P("ctx"),
        ),
        out_specs=(P("ctx", "head", None), P("ctx", "head"), P(("ctx", "head"), None), P("ctx")),
        check_vma=False,
    )
```

profile of v0, /device:TPU:1, one launch (start us, length us, event | category | flops | bytes accessed | tf_op | source)
XLA Modules:
  0.0 1145.0 jit_solution(16464791840338605670)
XLA Ops:
  12.5 197.3 %all-gather.3.cloned.1.call-done = bf16[96,128,576]{1,2,0:T(8,128)(2,1)} async-done(((bf16[6,128,576]{1,2,0:T(8,128)(2,1)}), bf16[96,128,576]{1,2,0:T(8,128)(2,1)}) %all-gather.3.cloned.1.call-update) | async-done | bytes 14155792 | tf_op jit(solution)/shard_map/all_gather | solution.py:58
  209.8 20.4 %copy.34 = bf16[96,128,576]{2,1,0:T(8,128)(2,1)} copy(bf16[96,128,576]{1,2,0:T(8,128)(2,1)} %all-gather.3.cloned.1.call-done) | data formatting | bytes 28311552 | tf_op jit(solution)/shard_map/while | solution.py:78
  230.2 69.1 %all-gather.5.cloned.1.call-done = bf16[96,128,128]{2,1,0:T(8,128)(2,1)} async-done(((bf16[6,128,128]{2,1,0:T(8,128)(2,1)}), bf16[96,128,128]{2,1,0:T(8,128)(2,1)}) %all-gather.5.cloned.1.call-update) | async-done | bytes 3145744 | tf_op jit(solution)/shard_map/all_gather | solution.py:59
  301.1 78.8 %while.29 = (s32[]{:T(128)}, bf16[16,128,576]{2,1,0:T(8,128)(2,1)}, bf16[16,128,128]{2,1,0:T(8,128)(2,1)S(1)}, s32[16]{0:T(128)S(1)}, bf16[96,128,576]{2,1,0:T(8...) while((s32[]{:T(128)}, bf16[16,128,576]{2,1,0:T(8,128)(2,1)}, ...), condition=%wide.region_3.4_spmd, body=%wide.region_0.3_spmd.sunk | while | flops 11 | bytes 393509 | solution.py:78
  380.7 148.7 %while.30 = (s32[]{:T(128)}, f32[256,2048]{1,0:T(8,128)}, bf16[256,8,576]{0,2,1:T(8,128)(2,1)}, bf16[2048,576]{1,0:T(8,128)(2,1)}, s32[256]{0:T(256)S(1)}, /*ind...) while((s32[]{:T(128)}, f32[256,2048]{1,0:T(8,128)}, ...), condition=%wide.region_12.13_spmd.clone, body=%wide.region_8.0_spmd.clone.sunk | while | flops 1219492864 | bytes 63663316 | solution.py:97
  385.7 4.4 broadcast_in_dim.112
  397.5 5.8 reshape.151
  403.5 11.6 %fusion.29 = f32[256,2048]{1,0:T(8,128)S(1)} fusion(f32[256,2,2048]{2,1,0:T(2,128)} %reshape.151, pred[256,2048]{1,0:T(8,128)(4,1)S(1)} %broadcast_compare_fusion.2, f32[256,2]{1,0:T(8,128)S(1)} %div.60, f32[256,2]{1,0:T(8,128)S(1)} %sub.102), kind=kLoop, calls=%fused_computation.7.clone.1 | loop fusion | flops 3670016 | bytes 6819840 | tf_op jit(solution)/shard_map/while/body/eval_jaxpr/reduce_sum | solution.py:95
  433.5 5.8 reshape.151
  439.4 11.6 %fusion.29 = f32[256,2048]{1,0:T(8,128)S(1)} fusion(f32[256,2,2048]{2,1,0:T(2,128)} %reshape.151, pred[256,2048]{1,0:T(8,128)(4,1)S(1)} %broadcast_compare_fusion.2, f32[256,2]{1,0:T(8,128)S(1)} %div.60, f32[256,2]{1,0:T(8,128)S(1)} %sub.102), kind=kLoop, calls=%fused_computation.7.clone.1 | loop fusion | flops 3670016 | bytes 6819840 | tf_op jit(solution)/shard_map/while/body/eval_jaxpr/reduce_sum | solution.py:95
  471.0 5.8 reshape.151
  477.0 11.6 %fusion.29 = f32[256,2048]{1,0:T(8,128)S(1)} fusion(f32[256,2,2048]{2,1,0:T(2,128)} %reshape.151, pred[256,2048]{1,0:T(8,128)(4,1)S(1)} %broadcast_compare_fusion.2, f32[256,2]{1,0:T(8,128)S(1)} %div.60, f32[256,2]{1,0:T(8,128)S(1)} %sub.102), kind=kLoop, calls=%fused_computation.7.clone.1 | loop fusion | flops 3670016 | bytes 6819840 | tf_op jit(solution)/shard_map/while/body/eval_jaxpr/reduce_sum | solution.py:95
  508.6 5.8 reshape.151
  514.6 11.6 %fusion.29 = f32[256,2048]{1,0:T(8,128)S(1)} fusion(f32[256,2,2048]{2,1,0:T(2,128)} %reshape.151, pred[256,2048]{1,0:T(8,128)(4,1)S(1)} %broadcast_compare_fusion.2, f32[256,2]{1,0:T(8,128)S(1)} %div.60, f32[256,2]{1,0:T(8,128)S(1)} %sub.102), kind=kLoop, calls=%fused_computation.7.clone.1 | loop fusion | flops 3670016 | bytes 6819840 | tf_op jit(solution)/shard_map/while/body/eval_jaxpr/reduce_sum | solution.py:95
  539.0 9.8 max.23
  548.8 11.4 multiply_reduce_fusion.1
  561.1 133.5 %all-reduce.3.cloned.1.call-done = (f32[256,2048]{1,0:T(8,128)}, f32[256,2048]{1,0:T(8,128)}) async-done(((f32[256,2048]{1,0:T(8,128)}, f32[256,2048]{1,0:T(8,128)}), (f32[256,2048]{1,0:T(8,128)}, f32[256,2048]{1,0:T(8,128)})) %all-reduce.3.cloned.1.call-update) | async-done | bytes 4194320 | tf_op jit(solution)/shard_map/psum | solution.py:106
  700.7 5.6 mul.81
  706.4 10.0 mul.82
  716.4 8.9 multiply_reduce_fusion
  725.3 6.4 copy.42
  742.0 7.3 dot_general.23
  749.3 6.7 fusion.3
  757.9 380.6 %reduce-scatter.2.cloned.1.call-done = f32[48,128]{1,0:T(8,128)} async-done(((f32[12288,128]{1,0:T(8,128)}), f32[48,128]{1,0:T(8,128)}) %reduce-scatter.2.cloned.1.call-update) | async-done | bytes 24592 | tf_op jit(solution)/shard_map/reduce_scatter | solution.py:120
  (172 shorter events, 206.9 us)
Async XLA Ops:
  7.2 522.2 %copy-start = (bf16[256,4,128]{2,1,0:T(4,128)(2,1)S(1)}, bf16[256,4,128]{2,1,0:T(4,128)(2,1)}, u32[]{:S(2)}) copy-start(bf16[256,4,128]{2,1,0:T(4,128)(2,1)} %param.15) | copy-start | bytes 786436
  7.2 3.8 copy-start.9
  7.2 202.6 %all-gather.3.cloned.1.call-start = ((), (), s32[]{:S(2)}) async-start(), calls=%async_computation.1 | async-start | bytes 15040512 | tf_op jit(solution)/shard_map/all_gather | solution.py:58
  10.1 289.1 %all-gather.5.cloned.1.call-start = ((), (), s32[]{:S(2)}) async-start(), calls=%async_computation.2 | async-start | bytes 3342336 | tf_op jit(solution)/shard_map/all_gather | solution.py:59
  10.9 683.7 %all-reduce.3.cloned.1.call-start = ((), (), s32[]{:S(2)}) async-start(), calls=%async_computation.4 | async-start | bytes 8388608 | tf_op jit(solution)/shard_map/psum | solution.py:106
  379.9 0.8 copy-start.5
  390.1 6.2 copy-start.2
  394.3 1.9 copy-start.1
  426.1 6.2 copy-start.2
  430.3 1.9 copy-start.1
  463.6 6.2 copy-start.2
  467.9 1.9 copy-start.1
  501.2 6.2 copy-start.2
  505.4 1.9 copy-start.1
  531.7 3.2 copy-start.3
  539.0 9.8 copy-start.8
  560.2 137.1 %copy-start.10 = (f32[256]{0:T(256)S(1)}, f32[256]{0:T(256)}, u32[]{:S(2)}) copy-start(f32[256]{0:T(256)} %param.19) | copy-start | bytes 3076
  560.2 578.3 %reduce-scatter.2.cloned.1.call-start = ((), (), s32[]{:S(2)}) async-start(), calls=%async_computation.3 | async-start | bytes 6316032 | tf_op jit(solution)/shard_map/reduce_scatter | solution.py:120
  694.5 2.2 copy-start.4
  694.5 2.9 copy-start.7
  742.0 7.3 copy-start.6
Sparse Core Ops, SparseCore 0:
  10.6 199.1 all-gather.2
  212.4 86.8 all-gather.4
  560.3 134.1 all-reduce.2
  742.1 396.3 reduce-scatter.1
where the time goes:
time: 1150 us; the launch traced here: 1140 us
  waiting for transfers between devices  781 us (68%)
  local copies, waits for them, and re-layouts  190 us (17%)
  other arithmetic  98.6 us (9%)
  loops' own time  31.9 us (3%)
  matrix products  29.3 us (3%)
  between operations  13.9 us (1%)
    reduce_scatter x1, waiting for transfers between devices, body(): lax.psum_scatter(dense_term, ('ctx', 'head'), scatter_dimension=0, tiled=...  381 us
    all_gather x1, waiting for transfers between devices, body(): latent_piece = lax.all_gather(latent_tiles, 'ctx', axis=0, tiled=True)  197 us
    psum x1, waiting for transfers between devices, body(): total_target, total_score = lax.psum((target_part, score_part), 'head')  133 us
    all_gather x1, waiting for transfers between devices, body(): index_piece = lax.all_gather(index_tiles, 'ctx', axis=0, tiled=True)  69.1 us
    reduce_sum x4, other arithmetic, add_heads(): return summed + jnp.sum(attend, axis=1)  46.3 us
    dynamic_update_slice x16, local copies, waits for them, and re-layouts, write_tile(): lax.dynamic_update_slice_in_dim(current[0], lax.dynamic_slice_in_dim(late...  25.6 us
    broadcast_in_dim x8, local copies, waits for them, and re-layouts, masked_softmax(): weights = jnp.where(allowed, jnp.exp(raw_scores - row_max), 0.0)  25.1 us
    reshape x4, local copies, waits for them, and re-layouts, add_heads(): raw_scores.reshape(query_rows, head_block, key_span)  23.3 us
  transfers between devices with their start and end apart: 4, of which 4 were waited for; matrix products, arithmetic and copies ran while one was open for 3% of the time, Pallas kernels for 0%

commit v1 on v0

v1 whole, which is shorter than its diff:
```python
import jax
import jax.numpy as jnp
from jax import lax
from jax.experimental import pallas as pl
from jax.experimental.pallas import tpu as pltpu
from jax.sharding import Mesh, PartitionSpec as P

TILE = 128
MLA_HEADS = 128
OWNER_MOST = 3
QROWS = 16
STRIPE = 8
VMEM = 50 * 1024 * 1024

CTX = ("z", "yh")
HEAD = ("yl", "x", "core")
ROWS = ("core", "yl", "x")
score_scale = 192.0 ** (-0.5)
far_below = -1e30


def allowed_keys(query_first, key_pos):
    rows = lax.broadcasted_iota(jnp.int32, (QROWS, key_pos.shape[1]), 0)
    return key_pos <= rows + query_first


def attend_kernel(place, query_first, *refs):
    pieces, (q_own, q_other, key_pos, target, index_keys, keys) = refs[:8], refs[8:]

    @pl.when(pl.program_id(0) == 0)
    def _():
        for i, piece in enumerate(pieces):
            for j in range(2):
                spot = pl.ds(pl.multiple_of(place[2 * i + j] * TILE, TILE), TILE)
                keys[spot, :] = piece[j]
                index_keys[spot, :] = piece[j, :, :TILE]

    latent = keys[:, TILE:]
    allowed = allowed_keys(query_first[0] + pl.program_id(0) * QROWS, key_pos[...])
    bias = jnp.where(allowed, 0.0, far_below)
    total = jnp.zeros(target.shape, jnp.float32)
    for q in (q_own, q_other):
        heads, rows, width = q.shape
        raw = lax.dot_general(
            q[...].reshape(heads * rows, width),
            latent,
            (((1,), (1,)), ((), ())),
            preferred_element_type=jnp.float32,
        ).reshape(heads, rows, latent.shape[0])
        raw = raw * score_scale + bias[None]
        top = jnp.max(raw, axis=-1, keepdims=True)
        weights = jnp.exp(raw - top)
        share = 1.0 / (jnp.sum(weights, axis=-1, keepdims=True) * MLA_HEADS)
        total = total + jnp.sum(weights * share, axis=0)
    target[...] = total


def index_logits(iq, keys, heads_step, step):
    rows = heads_step * QROWS
    block = iq[pl.ds(step * rows, rows), :]
    return lax.dot_general(
        block, keys[...], (((1,), (1,)), ((), ())), preferred_element_type=jnp.float32
    )


def score_kernel(iq, weight, keys, score):
    heads_step = 8
    rows = heads_step * QROWS
    span = keys.shape[0]
    total = jnp.zeros((QROWS, span), jnp.float32)
    for step in range(iq.shape[0] // rows):
        lifted = jnp.maximum(index_logits(iq, keys, heads_step, step), 0.0)
        lifted = lifted * weight[pl.ds(step * rows, rows), :]
        total = total + jnp.sum(lifted.reshape(heads_step, QROWS, span), axis=0)
    score[...] = total


def grad_kernel(
    query_first, parts, score, iq, iq_t, weight, keys, key_pos, loss_grad,
    query_grad, weight_grad, key_grad, loss, coef
):
    allowed = allowed_keys(query_first[0], key_pos[...])
    target = jnp.sum(parts[...], axis=0)
    masked = jnp.where(allowed, score[...], far_below)
    shifted = masked - jnp.max(masked, axis=-1, keepdims=True)
    weights = jnp.where(allowed, jnp.exp(shifted), 0.0)
    row_sum = jnp.sum(weights, axis=-1, keepdims=True)
    log_prob = shifted - jnp.log(row_sum)
    positive = target > 0
    self_term = jnp.where(positive, target * jnp.log(jnp.where(positive, target, 1.0)), 0.0)
    loss[...] = jnp.sum(
        jnp.where(allowed, self_term - target * log_prob, 0.0), axis=-1, keepdims=True
    )
    score_grad = loss_grad[...] * jnp.where(allowed, weights / row_sum - target, 0.0)
    heads_step = 8
    rows = heads_step * QROWS
    span = keys.shape[0]
    for step in range(iq.shape[0] // rows):
        spot = pl.ds(step * rows, rows)
        logits = index_logits(iq, keys, heads_step, step).reshape(heads_step, QROWS, span)
        scaled = score_grad[None] * weight[spot, :].reshape(heads_step, QROWS, 1)
        coef[spot, :] = (
            jnp.where(logits > 0, scaled, 0.0).astype(jnp.bfloat16).reshape(rows, span)
        )
        weight_grad[spot, :] = jnp.sum(
            score_grad[None] * jnp.maximum(logits, 0.0), axis=-1, keepdims=True
        ).reshape(rows, 1)
    query_grad[...] = jnp.dot(coef[...], keys[...], preferred_element_type=jnp.float32)
    flat = jnp.dot(iq_t[...], coef[...], preferred_element_type=jnp.float32)
    lanes = key_grad.shape[0] * key_grad.shape[1]
    for lane in range(lanes):
        key_grad[lane % 2, lane // 2] = flat[:, lane * TILE : (lane + 1) * TILE]


def whole(shape):
    return pl.BlockSpec(shape, lambda *_: (0,) * len(shape))


def one_hot_rows(table, block):
    a, b = table.shape
    eye = jnp.eye(block, dtype=table.dtype)
    return (table[:, None, :, None] * eye[None, :, None, :]).reshape(a * block, b * block)


def body(main_query, key_latent, index_query, index_key, index_weight, selection, loss_grad):
    bf16, f32 = jnp.bfloat16, jnp.float32
    ctx_index = lax.axis_index(CTX)
    ctx_count = lax.axis_size(CTX)
    lane = lax.axis_index(HEAD)
    lanes = lax.axis_size(HEAD)
    yl, x, core = lax.axis_index("yl"), lax.axis_index("x"), lax.axis_index("core")
    x_count = lax.axis_size("x")
    query_rows, main_local, lat_width = main_query.shape
    index_local, idx_width = index_query.shape[1:]
    key_tiles = key_latent.shape[0] // TILE
    sel_count = selection.shape[1]
    key_span = sel_count * TILE
    context = key_tiles * TILE * ctx_count
    width = idx_width + lat_width
    swap = [(0, 1), (1, 0)]

    owner = selection // key_tiles
    inner = selection % key_tiles
    earlier = jnp.tril(jnp.ones((sel_count, sel_count), jnp.int32), -1)
    rank = jnp.sum((owner[:, :, None] == owner[:, None, :]) * earlier[None], axis=2)
    ranks = jnp.arange(OWNER_MOST)
    picked = lax.dynamic_index_in_dim(selection, ctx_index, 0, keepdims=False)
    my_owner = lax.dynamic_index_in_dim(owner, ctx_index, 0, keepdims=False)
    my_rank = lax.dynamic_index_in_dim(rank, ctx_index, 0, keepdims=False)
    sent = jnp.any(
        (owner[:, None, :, None] == ctx_index)
        & (rank[:, None, :, None] == ranks[None, :, None, None])
        & (inner[:, None, :, None] == jnp.arange(key_tiles)[None, None, None, :]),
        axis=2,
    ).reshape(ctx_count * OWNER_MOST, key_tiles)
    got = (
        (my_owner[:, None, None] == jnp.arange(ctx_count)[None, :, None])
        & (my_rank[:, None, None] == ranks[None, None, :])
    ).reshape(sel_count, ctx_count * OWNER_MOST)

    own = jnp.concatenate([index_key, key_latent], axis=1)
    own = own.reshape(key_tiles, lanes, STRIPE, width)
    own = lax.dynamic_index_in_dim(own, lane, 1, keepdims=False).reshape(key_tiles * STRIPE, width)
    send = jnp.dot(one_hot_rows(sent.astype(bf16), STRIPE), own, preferred_element_type=bf16)
    arrived = lax.all_to_all(send, CTX, 0, 0, tiled=True)
    stripe = jnp.dot(one_hot_rows(got.astype(bf16), STRIPE), arrived, preferred_element_type=bf16)

    by_head = jnp.transpose(main_query, (1, 0, 2))
    half = query_rows // 2
    q_own = lax.dynamic_slice_in_dim(by_head, core * half, half, 1)
    q_other = lax.ppermute(
        lax.dynamic_slice_in_dim(by_head, (1 - core) * half, half, 1), "core", swap
    )

    near = jnp.stack([stripe, lax.ppermute(stripe, "yl", swap)])
    pieces = [near]
    for shift in range(1, x_count):
        ring = [(i, (i + shift) % x_count) for i in range(x_count)]
        pieces.append(lax.ppermute(near, "x", ring))
    pieces += [lax.ppermute(piece, "core", swap) for piece in pieces]
    place = jnp.stack(
        [
            ((yl ^ j) * x_count + (x - shift) % x_count) * 2 + (core ^ k)
            for k in range(2)
            for shift in range(x_count)
            for j in range(2)
        ]
    ).astype(jnp.int32)

    iq, _ = lax.optimization_barrier((index_query, stripe))
    iq = iq.reshape(lanes, QROWS, index_local, idx_width).transpose(0, 2, 1, 3)
    iq = lax.all_to_all(iq, ROWS, 0, 0, tiled=True).reshape(-1, idx_width)
    heads_all = lanes * index_local
    weight = lax.all_gather(index_weight, ROWS, axis=0, tiled=False)
    chunk = core * (lanes // 2) + yl * x_count + x
    weight = lax.dynamic_slice_in_dim(weight, chunk * QROWS, QROWS, 1)
    weight = weight.transpose(0, 2, 1).reshape(heads_all * QROWS, 1)
    grad_rows = lax.dynamic_slice_in_dim(loss_grad, chunk * QROWS, QROWS, 0).reshape(QROWS, 1)

    key_pos = (
        jnp.arange(lanes)[:, None, None] * STRIPE
        + picked[None, :, None] * TILE
        + jnp.arange(STRIPE)[None, None, :]
    ).reshape(1, key_span)
    block_first = context - query_rows * ctx_count + ctx_index * query_rows
    half_first = (block_first + core * half).reshape(1).astype(jnp.int32)
    chunk_first = (block_first + chunk * QROWS).reshape(1).astype(jnp.int32)

    params = pltpu.CompilerParams(vmem_limit_bytes=VMEM)
    q_spec = pl.BlockSpec((main_local, QROWS, lat_width), lambda i, *_: (0, i, 0))
    steps = half // QROWS
    target_part, index_keys = pl.pallas_call(
        attend_kernel,
        grid_spec=pltpu.PrefetchScalarGridSpec(
            num_scalar_prefetch=2,
            grid=(steps,),
            in_specs=[whole((2, TILE, width))] * 8 + [q_spec, q_spec, whole((1, key_span))],
            out_specs=[
                pl.BlockSpec((QROWS, key_span), lambda i, *_: (i, 0)),
                whole((key_span, idx_width)),
            ],
            scratch_shapes=[pltpu.VMEM((key_span, width), bf16)],
        ),
        out_shape=[
            jax.ShapeDtypeStruct((half, key_span), f32),
            jax.ShapeDtypeStruct((key_span, idx_width), bf16),
        ],
        compiler_params=params,
        cost_estimate=pl.CostEstimate(
            flops=4 * main_local * half * key_span * lat_width,
            bytes_accessed=8 * 2**20,
            transcendentals=2 * main_local * half * key_span,
        ),
        name="attend",
    )(place, half_first, *pieces, q_own, q_other, key_pos)

    target_parts = lax.all_to_all(target_part, ("yl", "x"), 0, 0, tiled=True)
    target_parts = target_parts.reshape(steps, QROWS, key_span)

    score = pl.pallas_call(
        score_kernel,
        out_shape=jax.ShapeDtypeStruct((QROWS, key_span), f32),
        compiler_params=params,
        cost_estimate=pl.CostEstimate(
            flops=2 * heads_all * QROWS * key_span * idx_width,
            bytes_accessed=2**20,
            transcendentals=0,
        ),
        name="score",
    )(iq, weight, index_keys)

    rows_all = heads_all * QROWS
    vmem = pl.BlockSpec(memory_space=pltpu.VMEM)
    query_grad, weight_grad, key_part, loss = pl.pallas_call(
        grad_kernel,
        in_specs=[pl.BlockSpec(memory_space=pltpu.SMEM)] + [vmem] * 8,
        out_shape=[
            jax.ShapeDtypeStruct((rows_all, idx_width), f32),
            jax.ShapeDtypeStruct((rows_all, 1), f32),
            jax.ShapeDtypeStruct((2, lanes // 2, idx_width, TILE), f32),
            jax.ShapeDtypeStruct((QROWS, 1), f32),
        ],
        scratch_shapes=[pltpu.VMEM((rows_all, key_span), bf16)],
        compiler_params=params,
        cost_estimate=pl.CostEstimate(
            flops=6 * rows_all * key_span * idx_width,
            bytes_accessed=4 * 2**20,
            transcendentals=0,
        ),
        name="grad",
    )(chunk_first, target_parts, score, iq, iq.T, weight, index_keys, key_pos, grad_rows)

    exact = lax.Precision.HIGHEST
    key_keep = lax.dynamic_index_in_dim(key_part, core, 0, keepdims=False)
    key_give = lax.dynamic_index_in_dim(key_part, 1 - core, 0, keepdims=False)
    key_sum = key_keep + lax.ppermute(key_give, "core", swap)
    key_sum = jnp.sum(
        lax.all_to_all(key_sum, ("yl", "x"), 0, 0, tiled=True), axis=0
    )
    back = lax.dot_general(
        one_hot_rows(got.astype(f32), STRIPE), key_sum, (((0,), (1,)), ((), ())), precision=exact
    )
    back = lax.all_to_all(back, CTX, 0, 0, tiled=True)
    own_blocks = lax.dot_general(
        one_hot_rows(sent.astype(f32), STRIPE), back, (((0,), (0,)), ((), ())), precision=exact
    ).reshape(key_tiles, STRIPE, idx_width)
    order = jnp.arange(lanes)
    natural = order % (lanes // 2) * 2 + order // (lanes // 2)
    goes = (jnp.arange(key_tiles)[None, :] * lanes + lane) // key_tiles == natural[:, None]
    key_send = jnp.sum(jnp.where(goes[:, :, None, None], own_blocks[None], 0.0), axis=1)

    small = jnp.concatenate(
        [
            weight_grad.reshape(lanes, index_local * QROWS),
            jnp.broadcast_to(loss.reshape(1, QROWS), (lanes, QROWS)),
            jnp.zeros((lanes, idx_width - (index_local + 1) * QROWS), f32),
        ],
        axis=1,
    ).reshape(lanes, 1, idx_width)
    packed = jnp.concatenate(
        [query_grad.reshape(lanes, index_local * QROWS, idx_width), key_send, small], axis=1
    )
    packed = lax.all_to_all(packed, ROWS, 0, 0, tiled=True)
    heads_rows = index_local * QROWS
    query_out = packed[:, :heads_rows].reshape(lanes, index_local, QROWS, idx_width)
    query_out = query_out.transpose(0, 2, 1, 3).reshape(query_rows, index_local, idx_width)
    blocks = packed[:, heads_rows : heads_rows + STRIPE]
    source = (lane * key_tiles + jnp.arange(key_tiles)) % lanes
    source = source % 2 * (lanes // 2) + source // 2
    comes = source[:, None] == order[None, :]
    key_out = jnp.sum(jnp.where(comes[:, :, None, None], blocks[None], 0.0), axis=1)
    key_out = key_out.reshape(key_tiles * STRIPE, idx_width)
    small = packed[:, heads_rows + STRIPE]
    weight_out = small[:, :heads_rows].reshape(lanes, index_local, QROWS)
    weight_out = weight_out.transpose(0, 2, 1).reshape(query_rows, index_local)
    loss_out = small[:, heads_rows : heads_rows + QROWS].reshape(query_rows)
    return (query_out, weight_out, key_out, loss_out)


def solution(mesh):
    fine = Mesh(mesh.devices.reshape(8, 2, 2, 4, 2), CTX + HEAD)
    return jax.shard_map(
        body,
        mesh=fine,
        in_specs=(
            P(CTX, HEAD, None),
            P(CTX, None),
            P(CTX, HEAD, None),
            P(CTX, None),
            P(CTX, HEAD),
            P(),
            P(CTX),
        ),
        out_specs=(P(CTX, HEAD, None), P(CTX, HEAD), P(CTX + HEAD, None), P(CTX)),
        check_vma=False,
    )
```

time: 1150 us -> 212 us (0.18)
  waiting for transfers between devices: 781 us -> 47.9 us
  local copies, waits for them, and re-layouts: 190 us -> 23.2 us
  other arithmetic: 98.6 us -> 10.3 us
  starting transfers between devices: 0.16 us -> 60.9 us
  blocking collectives: 0 us -> 37.8 us
  loops' own time: 31.9 us -> 0 us
  Pallas kernels: 0 us -> 26.2 us
  matrix products: 29.3 us -> 3.86 us
  between operations: 13.9 us -> 1.04 us
    reduce_scatter x1 -> x0, waiting for transfers between devices: 381 us -> none  [body(): lax.psum_scatter(dense_term, ('ctx', 'head'), scatter_dimension=0, tiled=...]
    all_gather x2 -> x0, waiting for transfers between devices: 266 us -> none  [the longest x1 197 us: body(): latent_piece = lax.all_gather(latent_tiles, 'ctx', axis=0, tiled=True)]
    psum x1 -> x0, waiting for transfers between devices: 133 us -> none  [body(): total_target, total_score = lax.psum((target_part, score_part), 'head')]
    reduce_sum x12 -> x4, other arithmetic: 74.9 us -> 1.4 us  [the longest x1 0.78 us: body(): jnp.sum(jnp.where(comes[:, :, None, None], blocks[None], 0.0), axis=1)]
    all_to_all x0 -> x6, waiting for transfers between devices: none -> 43.5 us  [the longest x1 12 us: body(): arrived = lax.all_to_all(send, CTX, 0, 0, tiled=True)]
    all_to_all x0 -> x6, starting transfers between devices: none -> 39.6 us  [the longest x1 11.8 us: body(): arrived = lax.all_to_all(send, CTX, 0, 0, tiled=True)]
    all_gather x0 -> x1, blocking collectives: none -> 37.8 us  [body(): weight = lax.all_gather(index_weight, ROWS, axis=0, tiled=False)]
    dynamic_update_slice x32 -> x0, local copies, waits for them, and re-layouts: 37.8 us -> none  [the longest x16 25.6 us: write_tile(): lax.dynamic_update_slice_in_dim(current[0], lax.dynamic_slice_in_dim(late...]
  transfers between devices with their start and end apart: 4 -> 16, of which waited for: 4 -> 6; matrix products, arithmetic and copies ran while one was open for 3% -> 10% of each run, Pallas kernels for 0% -> 10%
where the time goes in v1:
time: 212 us; the launch traced here: 211 us
  starting transfers between devices  60.9 us (29%)
  waiting for transfers between devices  47.9 us (23%)
  blocking collectives  37.8 us (18%)
  Pallas kernels  26.2 us (12%)
  local copies, waits for them, and re-layouts  23.2 us (11%)
  other arithmetic  10.3 us (5%)
  matrix products  3.86 us (2%)
    all_gather x1, blocking collectives, body(): weight = lax.all_gather(index_weight, ROWS, axis=0, tiled=False)  37.8 us
    pallas_call x1, Pallas kernels, body(): pl.pallas_call(attend_kernel, grid_spec=pltpu.PrefetchScalarGridSpec(num_...  20.4 us
    ppermute x4, starting transfers between devices, body(): pieces += [lax.ppermute(piece, 'core', swap) for piece in pieces]  14.9 us
    all_to_all x1, waiting for transfers between devices, body(): arrived = lax.all_to_all(send, CTX, 0, 0, tiled=True)  12 us
    all_to_all x1, waiting for transfers between devices, body(): packed = lax.all_to_all(packed, ROWS, 0, 0, tiled=True)  11.9 us
    all_to_all x1, starting transfers between devices, body(): arrived = lax.all_to_all(send, CTX, 0, 0, tiled=True)  11.8 us
    all_to_all x1, waiting for transfers between devices, body(): back = lax.all_to_all(back, CTX, 0, 0, tiled=True)  10.1 us
    all_to_all x1, waiting for transfers between devices, body(): lax.all_to_all(key_sum, ('yl', 'x'), 0, 0, tiled=True)  9.45 us
  transfers between devices with their start and end apart: 16, of which 6 were waited for; matrix products, arithmetic and copies ran while one was open for 10% of the time, Pallas kernels for 10%

profile of v1, /device:TPU:1, one launch (start us, length us, event | category | flops | bytes accessed | tf_op | source)
XLA Modules:
  0.0 211.2 jit_solution(6157421741802334698)
XLA Ops:
  6.4 11.8 %all-to-all-start = ((bf16[16,24,704]{2,1,0:T(8,128)(2,1)}), bf16[16,24,704]{2,1,0:T(8,128)(2,1)}, u32[]{:S(2)}, u32[]{:S(2)}) async-start(bf16[16,24,704]{2,1,0:T(8,128)(2,1)} %fusion), calls=%async_computation | async-start | bytes 1179648 | tf_op jit(solution)/shard_map/all_to_all | solution.py:165
  18.2 2.8 %dynamic-slice_bitcast_fusion = (bf16[8,128,576]{1,2,0:T(8,128)(2,1)}, bf16[128,8,576]{0,2,1:T(8,128)(2,1)S(1)}) fusion(bf16[256,8,576]{0,2,1:T(8,128)(2,1)} %param.7, s32[]{:T(128)S(6)} %select_n.163, s32[]{:T(128)S(6)} %select_n.162), kind=kLoop, calls=%fused_computation.2 | loop fusion | bytes 4718600 | tf_op jit(solution)/shard_map/dynamic_slice | solution.py:172
  23.0 1.8 mul.233
  24.7 12.0 %all-to-all-done = bf16[16,24,704]{2,1,0:T(8,128)(2,1)} async-done(((bf16[16,24,704]{2,1,0:T(8,128)(2,1)}), bf16[16,24,704]{2,1,0:T(8,128)(2,1)}, u32[]{:S(2)}, u32[]{:S(2)}) %all-to-all-start) | async-done | bytes 540704 | tf_op jit(solution)/shard_map/all_to_all | solution.py:165
  38.8 4.1 %collective-permute-done = bf16[128,704]{1,0:T(8,128)(2,1)S(1)} collective-permute-done((bf16[128,704]{1,0:T(8,128)(2,1)S(1)}, bf16[128,704]{1,0:T(8,128)(2,1)S(1)}, u32[]{:S(2)}, u32[]{:S(2)}) %collective-permute-start) | collective-permute-done | bytes 180256 | tf_op jit(solution)/shard_map/ppermute | solution.py:175
  44.3 2.4 %collective-permute-start.2 = (bf16[2,128,704]{2,1,0:T(8,128)(2,1)S(1)}, bf16[2,128,704]{2,1,0:T(8,128)(2,1)S(1)}, u32[]{:S(2)}, u32[]{:S(2)}) collective-permute-start(bf16[2,128,704]{2,1,0:T(8,128)(2,1)S(1)} %pad_maximum_fusion.2.refs_0_), channel_id=1, source_target_pairs={{0,4},{2,6},{4,0},{6,2},{1,5},{3,7},{5,1},{7,3},{8,12},{10,14},{12... | collective-permute-start | bytes 1081352 | tf_op jit(solution)/shard_map/ppermute | solution.py:179
  47.8 1.4 copy.113
  50.0 4.8 %collective-permute-start.4 = (bf16[2,128,704]{2,1,0:T(8,128)(2,1)S(1)}, bf16[2,128,704]{2,1,0:T(8,128)(2,1)S(1)}, u32[]{:S(2)}, u32[]{:S(2)}) collective-permute-start(bf16[2,128,704]{2,1,0:T(8,128)(2,1)S(1)} %pad_maximum_fusion.2.refs_0_), channel_id=1, source_target_pairs={{0,1},{1,0},{2,3},{3,2},{4,5},{5,4},{6,7},{7,6},{8,9},{9,8},{10,11... | collective-permute-start | bytes 1081352 | tf_op jit(solution)/shard_map/ppermute | solution.py:180
  54.8 4.9 %collective-permute-start.5 = (bf16[2,128,704]{2,1,0:T(8,128)(2,1)S(1)}, bf16[2,128,704]{2,1,0:T(8,128)(2,1)S(1)}, u32[]{:S(2)}, u32[]{:S(2)}) collective-permute-start(bf16[2,128,704]{2,1,0:T(8,128)(2,1)S(1)} %collective-permute-done.1.refs_1_), channel_id=1, source_target_pairs={{0,1},{1,0},{2,3},{3,2},{4,5},{5,4},{6,7},{7,6},{8,9},{9,8},{10,11... | collective-permute-start | bytes 1081352 | tf_op jit(solution)/shard_map/ppermute | solution.py:180
  60.0 5.2 %collective-permute-start.6 = (bf16[2,128,704]{2,1,0:T(8,128)(2,1)S(1)}, bf16[2,128,704]{2,1,0:T(8,128)(2,1)S(1)}, u32[]{:S(2)}, u32[]{:S(2)}) collective-permute-start(bf16[2,128,704]{2,1,0:T(8,128)(2,1)S(1)} %collective-permute-done.2.refs_2_), channel_id=1, source_target_pairs={{0,1},{1,0},{2,3},{3,2},{4,5},{5,4},{6,7},{7,6},{8,9},{9,8},{10,11... | collective-permute-start | bytes 1081352 | tf_op jit(solution)/shard_map/ppermute | solution.py:180
  67.3 4.2 %all-to-all-start.2 = ((bf16[16,4,16,128]{3,2,1,0:T(8,128)(2,1)}), bf16[16,4,16,128]{3,2,1,0:T(8,128)(2,1)S(1)}, u32[]{:S(2)}, u32[]{:S(2)}) async-start(bf16[16,4,16,128]{3,2,1,0:T(8,128)(2,1)} %copy.100), calls=%async_computation.2 | async-start | bytes 524288 | tf_op jit(solution)/shard_map/all_to_all | solution.py:192
  71.5 2.4 %copy.98.refs_9_ = bf16[8,128,576]{2,1,0:T(8,128)(2,1)} copy(bf16[8,128,576]{1,2,0:T(8,128)(2,1)} %collective-permute-done.8) | data formatting | bytes 2359296 | tf_op jit(solution)/shard_map/ppermute | solution.py:171
  73.9 20.4 %attend.1 = (f32[128,2048]{1,0:T(8,128)}, bf16[2048,128]{1,0:T(8,128)(2,1)S(1)}) custom-call(s32[16]{0:T(128)S(1)} %stack.76.place, s32[1]{0:T(128)} %bitcast.17.query_first, bf16[2,128,704]{2,1,0:T(8,128)(2,1)S(1)} %pad_maximum_fusion.2.refs_0_, bf16[2,128,704]{2,1,0:T(8,128)(2,1)S(1)} %collective-permute-done.1.refs_1_, ...), custom_call_target="tpu_custom_call" | custom-call | flops 4831838208 | bytes 8388608 | tf_op jit(solution)/shard_map/attend/pallas_call | solution.py:212
  95.2 5.2 %all-to-all-start.1 = ((f32[8,16,2048]{2,1,0:T(8,128)}), f32[8,16,2048]{2,1,0:T(8,128)S(1)}, u32[]{:S(2)}, u32[]{:S(2)}) async-start(f32[8,16,2048]{2,1,0:T(8,128)} %bitcast.112), calls=%async_computation.1 | async-start | bytes 2097152 | tf_op jit(solution)/shard_map/all_to_all | solution.py:237
  100.4 37.8 %all-gather = f32[4096,4]{0,1:T(4,128)S(1)} all-gather(f32[256,4]{0,1:T(4,128)S(1)} %copy-done.9), channel_id=2, replica_groups=mesh['z'=8,'yh'=2,'yl'=2,'x'=4,'core'=2] {'core','yl','x'}, dimensions={0}, use_global_device_ids=true | all-gather | bytes 69632 | tf_op jit(solution)/shard_map/all_gather | solution.py:194
  142.2 4.5 %grad.1 = (f32[1024,128]{1,0:T(8,128)S(1)}, f32[1024,1]{1,0:T(8,128)S(1)}, f32[2,8,128,128]{3,2,1,0:T(8,128)S(1)}, f32[16,1]{1,0:T(8,128)S(1)}) custom-call(s32[1]{0:T(128)} %bitcast.query_first, f32[8,16,2048]{2,1,0:T(8,128)} %copy-done.4, f32[16,2048]{1,0:T(8,128)S(1)} %score.1, bf16[1024,128]{1,0:T(8,128)(2,1)S(1)} %bitcast.106, ...), custom_call_target="tpu_custom_call" | custom-call | flops 1610612736 | bytes 4194304 | tf_op jit(solution)/shard_map/grad/pallas_call | solution.py:254
  147.8 1.9 broadcast_multiply_fusion
  149.7 3.2 %mul.253 = f32[128,384]{1,0:T(8,128)S(1)} reshape(f32[16,8,48,8]{3,2,1,0:T(8,128)} %broadcast_multiply_fusion) | data formatting | bytes 393216 | tf_op jit(solution)/shard_map/mul | solution.py:122
  154.1 5.4 %all-to-all-start.3 = ((f32[8,128,128]{2,1,0:T(8,128)}), f32[8,128,128]{2,1,0:T(8,128)S(1)}, u32[]{:S(2)}, u32[]{:S(2)}) async-start(f32[8,128,128]{2,1,0:T(8,128)} %bitcast_add_fusion), calls=%async_computation.3 | async-start | bytes 1048576 | tf_op jit(solution)/shard_map/all_to_all | solution.py:278
  160.3 9.5 %all-to-all-done.3 = f32[8,128,128]{2,1,0:T(8,128)S(1)} async-done(((f32[8,128,128]{2,1,0:T(8,128)}), f32[8,128,128]{2,1,0:T(8,128)S(1)}, u32[]{:S(2)}, u32[]{:S(2)}) %all-to-all-start.3) | async-done | bytes 524320 | tf_op jit(solution)/shard_map/all_to_all | solution.py:278
  170.8 7.0 %all-to-all-start.4 = ((f32[16,24,128]{2,1,0:T(8,128)}), f32[16,24,128]{2,1,0:T(8,128)S(1)}, u32[]{:S(2)}, u32[]{:S(2)}) async-start(f32[16,24,128]{2,1,0:T(8,128)} %fusion.6), calls=%async_computation.4 | async-start | bytes 393216 | tf_op jit(solution)/shard_map/all_to_all | solution.py:283
  178.4 10.1 %all-to-all-done.4 = f32[16,24,128]{2,1,0:T(8,128)S(1)} async-done(((f32[16,24,128]{2,1,0:T(8,128)}), f32[16,24,128]{2,1,0:T(8,128)S(1)}, u32[]{:S(2)}, u32[]{:S(2)}) %all-to-all-start.4) | async-done | bytes 196640 | tf_op jit(solution)/shard_map/all_to_all | solution.py:283
  189.8 6.1 %all-to-all-start.5 = ((f32[16,73,128]{2,1,0:T(8,128)}), f32[16,73,128]{2,1,0:T(8,128)S(1)}, u32[]{:S(2)}, u32[]{:S(2)}) async-start(f32[16,73,128]{2,1,0:T(8,128)} %pad_maximum_fusion.1), calls=%async_computation.5 | async-start | bytes 1310720 | tf_op jit(solution)/shard_map/all_to_all | solution.py:303
  196.0 11.9 %all-to-all-done.5 = f32[16,73,128]{2,1,0:T(8,128)S(1)} async-done(((f32[16,73,128]{2,1,0:T(8,128)}), f32[16,73,128]{2,1,0:T(8,128)S(1)}, u32[]{:S(2)}, u32[]{:S(2)}) %all-to-all-start.5) | async-done | bytes 598048 | tf_op jit(solution)/shard_map/all_to_all | solution.py:303
  (117 shorter events, 29.3 us)
Async XLA Ops:
  0.6 138.0 %copy-start = (f32[256]{0:T(256)S(1)}, f32[256]{0:T(256)}, u32[]{:S(2)}) copy-start(f32[256]{0:T(256)} %param.13) | copy-start | bytes 3076
  0.6 3.8 %copy-start.5 = (bf16[768,576]{0,1:T(8,128)(2,1)S(1)}, bf16[768,576]{0,1:T(8,128)(2,1)}, u32[]{:S(2)}) copy-start(bf16[768,576]{0,1:T(8,128)(2,1)} %param.8) | copy-start | bytes 2654212
  6.4 30.3 %all-to-all-start = ((bf16[16,24,704]{2,1,0:T(8,128)(2,1)}), bf16[16,24,704]{2,1,0:T(8,128)(2,1)}, u32[]{:S(2)}, u32[]{:S(2)}) async-start(bf16[16,24,704]{2,1,0:T(8,128)(2,1)} %fusion), calls=%async_computation | async-start | bytes 1179648 | tf_op jit(solution)/shard_map/all_to_all | solution.py:165
  21.1 50.4 %collective-permute-start.8 = (bf16[8,128,576]{1,2,0:T(8,128)(2,1)}, bf16[8,128,576]{1,2,0:T(8,128)(2,1)}, u32[]{:S(2)}, u32[]{:S(2)}) collective-permute-start(bf16[8,128,576]{1,2,0:T(8,128)(2,1)} %get-tuple-element.20), channel_id=1, source_target_pairs={{0,1},{1,0},{2,3},{3,2},{4,5},{5,4},{6,7},{7,6},{8,9},{9,8},{10,11... | collective-permute-start | bytes 3538952 | tf_op jit(solution)/shard_map/ppermute | solution.py:171
  38.3 4.6 %collective-permute-start = (bf16[128,704]{1,0:T(8,128)(2,1)S(1)}, bf16[128,704]{1,0:T(8,128)(2,1)S(1)}, u32[]{:S(2)}, u32[]{:S(2)}) collective-permute-start(bf16[128,704]{1,0:T(8,128)(2,1)S(1)} %copy.95), channel_id=1, source_target_pairs={{0,8},{8,0},{1,9},{9,1},{2,10},{10,2},{3,11},{11,3},{4,12},{12,4},... | collective-permute-start | bytes 540680 | tf_op jit(solution)/shard_map/ppermute | solution.py:175
  43.0 11.8 %collective-permute-start.1 = (bf16[2,128,704]{2,1,0:T(8,128)(2,1)S(1)}, bf16[2,128,704]{2,1,0:T(8,128)(2,1)S(1)}, u32[]{:S(2)}, u32[]{:S(2)}) collective-permute-start(bf16[2,128,704]{2,1,0:T(8,128)(2,1)S(1)} %pad_maximum_fusion.2.refs_0_), channel_id=1, source_target_pairs={{0,2},{2,4},{4,6},{6,0},{1,3},{3,5},{5,7},{7,1},{8,10},{10,12},{12... | collective-permute-start | bytes 1081352 | tf_op jit(solution)/shard_map/ppermute | solution.py:179
  44.3 15.7 %collective-permute-start.2 = (bf16[2,128,704]{2,1,0:T(8,128)(2,1)S(1)}, bf16[2,128,704]{2,1,0:T(8,128)(2,1)S(1)}, u32[]{:S(2)}, u32[]{:S(2)}) collective-permute-start(bf16[2,128,704]{2,1,0:T(8,128)(2,1)S(1)} %pad_maximum_fusion.2.refs_0_), channel_id=1, source_target_pairs={{0,4},{2,6},{4,0},{6,2},{1,5},{3,7},{5,1},{7,3},{8,12},{10,14},{12... | collective-permute-start | bytes 1081352 | tf_op jit(solution)/shard_map/ppermute | solution.py:179
  46.7 18.5 %collective-permute-start.3 = (bf16[2,128,704]{2,1,0:T(8,128)(2,1)S(1)}, bf16[2,128,704]{2,1,0:T(8,128)(2,1)S(1)}, u32[]{:S(2)}, u32[]{:S(2)}) collective-permute-start(bf16[2,128,704]{2,1,0:T(8,128)(2,1)S(1)} %pad_maximum_fusion.2.refs_0_), channel_id=1, source_target_pairs={{0,6},{2,0},{4,2},{6,4},{1,7},{3,1},{5,3},{7,5},{8,14},{10,8},{12,... | collective-permute-start | bytes 1081352 | tf_op jit(solution)/shard_map/ppermute | solution.py:179
  50.0 23.9 %collective-permute-start.4 = (bf16[2,128,704]{2,1,0:T(8,128)(2,1)S(1)}, bf16[2,128,704]{2,1,0:T(8,128)(2,1)S(1)}, u32[]{:S(2)}, u32[]{:S(2)}) collective-permute-start(bf16[2,128,704]{2,1,0:T(8,128)(2,1)S(1)} %pad_maximum_fusion.2.refs_0_), channel_id=1, source_target_pairs={{0,1},{1,0},{2,3},{3,2},{4,5},{5,4},{6,7},{7,6},{8,9},{9,8},{10,11... | collective-permute-start | bytes 1081352 | tf_op jit(solution)/shard_map/ppermute | solution.py:180
  54.8 19.1 %collective-permute-start.5 = (bf16[2,128,704]{2,1,0:T(8,128)(2,1)S(1)}, bf16[2,128,704]{2,1,0:T(8,128)(2,1)S(1)}, u32[]{:S(2)}, u32[]{:S(2)}) collective-permute-start(bf16[2,128,704]{2,1,0:T(8,128)(2,1)S(1)} %collective-permute-done.1.refs_1_), channel_id=1, source_target_pairs={{0,1},{1,0},{2,3},{3,2},{4,5},{5,4},{6,7},{7,6},{8,9},{9,8},{10,11... | collective-permute-start | bytes 1081352 | tf_op jit(solution)/shard_map/ppermute | solution.py:180
  60.0 13.9 %collective-permute-start.6 = (bf16[2,128,704]{2,1,0:T(8,128)(2,1)S(1)}, bf16[2,128,704]{2,1,0:T(8,128)(2,1)S(1)}, u32[]{:S(2)}, u32[]{:S(2)}) collective-permute-start(bf16[2,128,704]{2,1,0:T(8,128)(2,1)S(1)} %collective-permute-done.2.refs_2_), channel_id=1, source_target_pairs={{0,1},{1,0},{2,3},{3,2},{4,5},{5,4},{6,7},{7,6},{8,9},{9,8},{10,11... | collective-permute-start | bytes 1081352 | tf_op jit(solution)/shard_map/ppermute | solution.py:180
  65.2 8.7 %collective-permute-start.7 = (bf16[2,128,704]{2,1,0:T(8,128)(2,1)S(1)}, bf16[2,128,704]{2,1,0:T(8,128)(2,1)S(1)}, u32[]{:S(2)}, u32[]{:S(2)}) collective-permute-start(bf16[2,128,704]{2,1,0:T(8,128)(2,1)S(1)} %collective-permute-done.3.refs_3_), channel_id=1, source_target_pairs={{0,1},{1,0},{2,3},{3,2},{4,5},{5,4},{6,7},{7,6},{8,9},{9,8},{10,11... | collective-permute-start | bytes 1081352 | tf_op jit(solution)/shard_map/ppermute | solution.py:180
  67.3 27.9 %all-to-all-start.2 = ((bf16[16,4,16,128]{3,2,1,0:T(8,128)(2,1)}), bf16[16,4,16,128]{3,2,1,0:T(8,128)(2,1)S(1)}, u32[]{:S(2)}, u32[]{:S(2)}) async-start(bf16[16,4,16,128]{3,2,1,0:T(8,128)(2,1)} %copy.100), calls=%async_computation.2 | async-start | bytes 524288 | tf_op jit(solution)/shard_map/all_to_all | solution.py:192
  95.2 5.2 %copy-start.9 = (f32[256,4]{0,1:T(4,128)S(1)}, f32[256,4]{0,1:T(4,128)}, u32[]{:S(2)}) copy-start(f32[256,4]{0,1:T(4,128)} %param.11) | copy-start | bytes 12292
  95.2 43.8 %copy-start.2 = (bf16[2048,128]{1,0:T(8,128)(2,1)S(1)}, bf16[2048,128]{1,0:T(8,128)(2,1)}, u32[]{:S(2)}) copy-start(bf16[2048,128]{1,0:T(8,128)(2,1)} %copy-done.1) | copy-start | bytes 1572868
  95.2 45.0 %all-to-all-start.1 = ((f32[8,16,2048]{2,1,0:T(8,128)}), f32[8,16,2048]{2,1,0:T(8,128)S(1)}, u32[]{:S(2)}, u32[]{:S(2)}) async-start(f32[8,16,2048]{2,1,0:T(8,128)} %bitcast.112), calls=%async_computation.1 | async-start | bytes 2097152 | tf_op jit(solution)/shard_map/all_to_all | solution.py:237
  140.2 1.0 copy-start.4
  141.2 1.0 copy-start.3
  142.2 5.4 %copy-start.7 = (f32[16,16,3]{0,2,1:T(4,128)S(1)}, f32[16,16,3]{0,2,1:T(4,128)}, u32[]{:S(2)}) copy-start(f32[16,16,3]{0,2,1:T(4,128)} %get-tuple-element.24) | copy-start | bytes 9220
  147.6 5.6 %collective-permute-start.9 = (f32[8,128,128]{2,1,0:T(8,128)}, f32[8,128,128]{2,1,0:T(8,128)S(1)}, u32[]{:S(2)}, u32[]{:S(2)}) collective-permute-start(f32[8,128,128]{2,1,0:T(8,128)} %dynamic-slice_bitcast_fusion.1), channel_id=1, source_target_pairs={{0,1},{1,0},{2,3},{3,2},{4,5},{5,4},{6,7},{7,6},{8,9},{9,8},{10,11... | collective-permute-start | bytes 1572872 | tf_op jit(solution)/shard_map/ppermute | solution.py:276
  149.7 3.3 %copy-start.8 = (f32[16,3,6]{0,2,1:T(8,128)S(1)}, f32[16,3,6]{0,2,1:T(8,128)}, u32[]{:S(2)}) copy-start(f32[16,3,6]{0,2,1:T(8,128)} %get-tuple-element.22) | copy-start | bytes 3460
  154.1 15.7 %all-to-all-start.3 = ((f32[8,128,128]{2,1,0:T(8,128)}), f32[8,128,128]{2,1,0:T(8,128)S(1)}, u32[]{:S(2)}, u32[]{:S(2)}) async-start(f32[8,128,128]{2,1,0:T(8,128)} %bitcast_add_fusion), calls=%async_computation.3 | async-start | bytes 1048576 | tf_op jit(solution)/shard_map/all_to_all | solution.py:278
  170.8 17.7 %all-to-all-start.4 = ((f32[16,24,128]{2,1,0:T(8,128)}), f32[16,24,128]{2,1,0:T(8,128)S(1)}, u32[]{:S(2)}, u32[]{:S(2)}) async-start(f32[16,24,128]{2,1,0:T(8,128)} %fusion.6), calls=%async_computation.4 | async-start | bytes 393216 | tf_op jit(solution)/shard_map/all_to_all | solution.py:283
  189.8 18.1 %all-to-all-start.5 = ((f32[16,73,128]{2,1,0:T(8,128)}), f32[16,73,128]{2,1,0:T(8,128)S(1)}, u32[]{:S(2)}, u32[]{:S(2)}) async-start(f32[16,73,128]{2,1,0:T(8,128)} %pad_maximum_fusion.1), calls=%async_computation.5 | async-start | bytes 1310720 | tf_op jit(solution)/shard_map/all_to_all | solution.py:303
  (2 other events, 1.8 us)
